TPU v7x, 32 devices: a whole 2x2x4 slice. The times are simulated.
32 devices in a mesh: seq: 16 (over z, y, x), chan: 2 (over core).
Axes of the slice: x: 2, y: 2, z: 4, core: 2. Of those that a mesh axis runs over, the one named last changes fastest.
Arguments:
- signal: bfloat16 [2048, 2048], P('seq', 'chan'), may hold values from -6 to 6
- cotangent: bfloat16 [2048, 2048], P('seq', 'chan'), may hold values from -6 to 6
- w_proj: bfloat16 [2048, 560], P('chan'), may hold values from -0.013671875 to 0.013671875
- w_delta: bfloat16 [2, 256, 2048], P(None, None, 'chan'), may hold values from -3.5625 to 3.5625
- delta_bias: float32 [2, 2048], P(None, 'chan'), may hold values from -1 to 0.5
- decay_log: float32 [2, 12, 2048], P(None, None, 'chan'), may hold values from -12 to -3, as said below
- skip_gain: float32 [2048], P('chan'), may hold values from 0.5 to 1.5
Outputs:
- layer_out: bfloat16 [2048, 2048], P('seq', 'chan')
- signal_grad: bfloat16 [2048, 2048], P('seq', 'chan')
Inputs may be any that keep to these rules, and one draw needn't show every extreme that they name: `decay_log`: each entry is the logarithm of a positive decay rate.
All inputs are finite; a program needn't handle non-finite values.
Results may differ from a plain program's by a relative error of at most 0.0085.
Values may be sent and summed in bfloat16 or wider, within the bound.
A program may use at most 64 MiB of HBM per device.

v0:
```python
import functools
import math

import jax
import jax.numpy as jnp
from jax import lax
from jax.experimental import pallas as pl
from jax.experimental.pallas import tpu as pltpu
from jax.sharding import PartitionSpec as P

SUB = 8
LANES = 128
MESH = pl.DeviceIdType.MESH
LIMIT = 56 * 1024 * 1024
F32 = jnp.float32
BF16 = jnp.bfloat16
LOG2E = math.log2(math.e)
NT = (((1,), (1,)), ((), ()))


def mm(a, b):
    return jnp.dot(a, b, preferred_element_type=F32)


def order_matrix(rows, back):
    steps = rows // SUB
    work, token = (1, 0) if back else (0, 1)
    r = lax.broadcasted_iota(jnp.int32, (rows, rows), work)
    t = lax.broadcasted_iota(jnp.int32, (rows, rows), token)
    return jnp.where(t == (r & (SUB - 1)) * steps + (r >> 3), 1.0, 0.0).astype(BF16)


def tile_rows(step):
    return pl.ds(pl.multiple_of(step * SUB, SUB), SUB)


def tile_cols(block):
    return pl.ds(pl.multiple_of(block * LANES, LANES), LANES)


def softplus(x):
    return jnp.maximum(x, 0.0) + jnp.log1p(jnp.exp(-jnp.abs(x)))


def fill_rates(log_ref, rate_ref):
    depth = log_ref.shape[0]
    for k in range(2):
        rate = jnp.exp(log_ref[:, k]) * (-LOG2E)
        for n in range(depth):
            rate_ref[k * depth + n] = jnp.broadcast_to(rate[n : n + 1], rate_ref.shape[1:])


def fill_gates(gates, gate_ref):
    for m in range(gate_ref.shape[0]):
        gate_ref[m] = jnp.broadcast_to(gates[:, m : m + 1], gate_ref.shape[1:])


def greet(places):
    barrier = pltpu.get_barrier_semaphore()
    for place in places:
        pl.semaphore_signal(barrier, inc=1, device_id=place, device_id_type=MESH)
    return barrier, len(places)


def share_and_sum(peers, slots_ref, send_sem, recv_sem, greeting):
    me = lax.axis_index("chan")
    pl.semaphore_wait(*greeting)
    sends = []
    for o in range(1, peers):
        copy = pltpu.make_async_remote_copy(
            src_ref=slots_ref.at[me],
            dst_ref=slots_ref.at[me],
            send_sem=send_sem.at[o - 1],
            recv_sem=recv_sem.at[o - 1],
            device_id={"chan": lax.rem(me + o, peers)},
            device_id_type=MESH,
        )
        copy.start()
        sends.append(copy)
    for o in range(1, peers):
        origin = lax.rem(me + peers - o, peers)
        pltpu.make_async_remote_copy(
            src_ref=slots_ref.at[origin],
            dst_ref=slots_ref.at[origin],
            send_sem=send_sem.at[o - 1],
            recv_sem=recv_sem.at[o - 1],
            device_id={"chan": origin},
            device_id_type=MESH,
        ).wait_recv()
    total = slots_ref[0]
    for p in range(1, peers):
        total = total + slots_ref[p]
    return total, sends


def chan_places(peers):
    me = lax.axis_index("chan")
    return [{"chan": lax.rem(me + o, peers)} for o in range(1, peers)]


def project_kernel(
    peers, sig_ref, cot_ref, w_ref, proj_ref, sigp_ref, cotp_ref, slots_ref, send_sem, recv_sem
):
    greeting = greet(chan_places(peers))
    me = lax.axis_index("chan")
    order = order_matrix(sig_ref.shape[0], False)
    sig = mm(order, sig_ref[...]).astype(BF16)
    slots_ref[me] = lax.dot_general(sig, w_ref[...], NT, preferred_element_type=F32)
    sigp_ref[...] = sig
    cotp_ref[...] = mm(order, cot_ref[...]).astype(BF16)
    total, sends = share_and_sum(peers, slots_ref, send_sem, recv_sem, greeting)
    proj_ref[...] = total.astype(BF16)
    for copy in sends:
        copy.wait_send()


def radices(count):
    found = []
    while count % 4 == 0 and count > 4:
        small = count % 16 == 0 and not found
        found += [2, 2] if small else [4]
        count //= 4
    return found + ([count] if count > 1 else [])


def place_at(me, stride, radix, shift):
    digit = lax.rem(me // stride, radix)
    return me + (lax.rem(digit + shift, radix) - digit) * stride


def exchange_kernel(
    levels, log_ref, dev_ref, total_ref, enter_ref,
    part_refs, span_refs, run_ref, wide_ref, send_sem, recv_sem,
):
    me = lax.axis_index("seq")
    depth = log_ref.shape[0]
    places = []
    stride = 1
    for radix in levels:
        places += [{"seq": place_at(me, stride, radix, o)} for o in range(1, radix)]
        stride *= radix
    greeting = greet(places)
    rates = jnp.concatenate([log_ref[:, 0], log_ref[:, 1]], 0)
    rates = jnp.exp(rates) * (-LOG2E)
    upper = lax.broadcasted_iota(jnp.int32, rates.shape, 0) < depth

    def power(span):
        return jnp.exp2(rates * jnp.where(upper, span[0:1], span[1:2]))

    enter_ref[...] = jnp.zeros_like(enter_ref)
    wide_ref[...] = jnp.zeros_like(wide_ref)
    pl.semaphore_wait(*greeting)
    stride = 1
    base = 0
    sends = []
    for level, radix in enumerate(levels):
        last = level == len(levels) - 1
        digit = lax.rem(me // stride, radix)
        parts, spans = part_refs[level], span_refs[level]
        if level == 0:
            parts[digit] = dev_ref[...]
            spans[digit] = total_ref[...]

        def copies(slot, place, o, group):
            at = base + 2 * (o - 1)
            block = parts.at[slot, group] if last else parts.at[slot]
            return [
                pltpu.make_async_remote_copy(
                    src_ref=ref,
                    dst_ref=ref,
                    send_sem=send_sem.at[at + i],
                    recv_sem=recv_sem.at[at + i],
                    device_id={"seq": place},
                    device_id_type=MESH,
                )
                for i, ref in enumerate((block, spans.at[slot]))
            ]

        for o in range(1, radix):
            peer = lax.rem(digit + o, radix)
            group = jnp.where(peer > digit, 0, 1)
            for copy in copies(digit, place_at(me, stride, radix, o), o, group):
                copy.start()
                sends.append(copy)
        for o in range(1, radix):
            peer = lax.rem(digit + radix - o, radix)
            group = jnp.where(peer < digit, 0, 1)
            for copy in copies(peer, place_at(me, stride, radix, radix - o), o, group):
                copy.wait_recv()

        for group in range(2):
            run_ref[...] = jnp.zeros_like(run_ref)
            far = jnp.zeros(total_ref.shape, F32)
            old = power(wide_ref[group])
            for step in range(radix):
                d = step if group == 0 else radix - 1 - step
                mine = digit == d

                @pl.when(mine)
                def _(group=group, far=far, old=old):
                    enter_ref[group] = enter_ref[group] + old * run_ref[...]
                    wide_ref[group] = wide_ref[group] + far

                ahead = (digit > d) if group == 0 else (digit < d)
                if last:

                    @pl.when(ahead)
                    def _(d=d, group=group):
                        run_ref[...] = run_ref[...] * power(spans[d]) + parts[d, group].astype(F32)

                else:
                    run_ref[...] = run_ref[...] * power(spans[d]) + parts[d, group].astype(F32)
                    far = far + spans[d]
            if not last:
                following = lax.rem(me // (stride * radix), levels[level + 1])
                part_refs[level + 1][following, group] = run_ref[...].astype(BF16)
                if group == 0:
                    span_refs[level + 1][following] = far
        base += 2 * (radix - 1)
        stride *= radix
    for copy in sends:
        copy.wait_send()


def sublane_scan(decay, value, rising):
    sub = lax.broadcasted_iota(jnp.int32, value.shape, 0)
    shift = 1
    while shift < SUB:
        amount = shift if rising else SUB - shift
        has = (sub >= shift) if rising else (sub < SUB - shift)
        value = value + decay * jnp.where(has, pltpu.roll(value, amount, 0), 0.0)
        decay = decay * jnp.where(has, pltpu.roll(decay, amount, 0), 1.0)
        shift *= 2
    edge = (sub >= 1) if rising else (sub < SUB - 1)
    before = jnp.where(edge, pltpu.roll(value, 1 if rising else SUB - 1, 0), 0.0)
    last = SUB - 1 if rising else 0
    return before, value[last : last + 1]


def summary_kernel(
    proj_ref, sigp_ref, cotp_ref, wd_ref, bias_ref, log_ref,
    pre_ref, entry_ref, span_ref, dev_ref, total_ref,
    delta_ref, sig_ref, cot_ref, gate_ref, rate_ref, edge_ref,
):
    rows, width = sigp_ref.shape
    depth = log_ref.shape[0]
    rank = wd_ref.shape[1]
    steps = rows // SUB
    proj = proj_ref[...]
    for k in range(2):
        pre = mm(proj[:, k * rank : (k + 1) * rank], wd_ref[k]) + bias_ref[k : k + 1, :]
        pre_ref[k] = pre
        delta_ref[k] = softplus(pre)
    sig_ref[...] = sigp_ref[...].astype(F32)
    cot_ref[...] = cotp_ref[...].astype(F32)
    fill_gates(proj[:, 2 * rank :].astype(F32), gate_ref)
    fill_rates(log_ref, rate_ref)
    half = (depth + 1) // 2

    def block_body(block, _):
        cols = tile_cols(block)
        zero = jnp.zeros((SUB, LANES), F32)
        for k in range(2):
            for first in range(0, depth, half):
                ns = range(first, min(first + half, depth))

                def step_body(i, carry, ns=ns, k=k):
                    span, state, power, adjoint = carry
                    for u in range(2):
                        at = i * 2 + u
                        here = tile_rows(at if k == 0 else steps - 1 - at)
                        delta = delta_ref[k, here, cols]
                        weight = delta * sig_ref[here, cols]
                        cot = cot_ref[here, cols]
                        span = span + delta
                        new = ([], [], [])
                        for j, n in enumerate(ns):
                            a = jnp.exp2(delta * rate_ref[k * depth + n, :, cols])
                            p = a * power[j]
                            new[0].append(
                                a * state[j] + weight * gate_ref[2 * k * depth + n, here, :]
                            )
                            new[1].append(p)
                            new[2].append(
                                adjoint[j] + p * (cot * gate_ref[(2 * k + 1) * depth + n, here, :])
                            )
                        state, power, adjoint = (tuple(x) for x in new)
                    return span, state, power, adjoint

                zeros = (zero,) * len(ns)
                ones = (jnp.ones((SUB, LANES), F32),) * len(ns)
                span, state, power, adjoint = lax.fori_loop(
                    0, steps // 2, step_body, (zero, zeros, ones, zeros)
                )
                if first == 0:
                    one = jnp.ones((SUB, LANES), F32)
                    below, whole = sublane_scan(one, span, True)
                    above, _unused = sublane_scan(one, span, False)
                    span_ref[0, k, :, cols] = below
                    span_ref[1, k, :, cols] = above
                    total_ref[k : k + 1, cols] = whole
                for j, n in enumerate(ns):
                    row = k * depth + n
                    for kind, value in ((0, state[j]), (1, adjoint[j])):
                        group = k ^ kind
                        before, edge = sublane_scan(power[j], value, group == 0)
                        entry_ref[group, row, :, cols] = before
                        edge_ref[group, row : row + 1, cols] = edge
        return 0

    lax.fori_loop(0, width // LANES, block_body, 0)
    dev_ref[...] = edge_ref[...].astype(BF16)


def scan_kernel(
    proj_ref, sigp_ref, cotp_ref, pre_ref, wd_ref, log_ref, skip_ref,
    entry_ref, span_ref, enter_ref,
    out_ref, part_ref, base_ref,
    delta_ref, sig_ref, cot_ref, gate_ref, rate_ref,
    core_ref, gsig_ref, gpre_ref, acc_ref, keep_ref, decay_ref,
):
    rows, width = sigp_ref.shape
    depth = log_ref.shape[0]
    rank = wd_ref.shape[1]
    steps = rows // SUB
    for k in range(2):
        delta_ref[k] = softplus(pre_ref[k])
    sig_ref[...] = sigp_ref[...].astype(F32)
    cot_ref[...] = cotp_ref[...].astype(F32)
    fill_gates(proj_ref[:, 2 * rank :].astype(F32), gate_ref)
    fill_rates(log_ref, rate_ref)
    acc_ref[...] = jnp.zeros_like(acc_ref)
    core_ref[...] = jnp.zeros_like(core_ref)
    gsig_ref[...] = jnp.zeros_like(gsig_ref)

    def start(group, k, n, cols):
        row = k * depth + n
        decay = jnp.exp2(rate_ref[row, :, cols] * span_ref[group, k, :, cols])
        return entry_ref[group, row, :, cols] + decay * enter_ref[group, row : row + 1, cols]

    def block_body(block, _):
        cols = tile_cols(block)
        for k in range(2):
            gate_in = 2 * k * depth
            gate_out = gate_in + depth

            def forward(i, states, k=k, gate_in=gate_in, gate_out=gate_out):
                for u in range(2):
                    at = i * 2 + u
                    at = at if k == 0 else steps - 1 - at
                    here = tile_rows(at)
                    delta = delta_ref[k, here, cols]
                    weight = delta * sig_ref[here, cols]
                    cot = cot_ref[here, cols]
                    core = core_ref[here, cols]
                    new = []
                    for n in range(depth):
                        a = jnp.exp2(delta * rate_ref[k * depth + n, :, cols])
                        kept = a * states[n]
                        h = kept + weight * gate_ref[gate_in + n, here, :]
                        decay_ref[at, n] = a
                        keep_ref[at, n] = kept
                        core = core + gate_ref[gate_out + n, here, :] * h
                        lane = slice((gate_out + n) * LANES, (gate_out + n + 1) * LANES)
                        acc_ref[here, lane] += cot * h
                        new.append(h)
                    core_ref[here, cols] = core
                    states = tuple(new)
                return states

            lax.fori_loop(
                0, steps // 2, forward, tuple(start(k, k, n, cols) for n in range(depth))
            )

            def backward(i, carried, k=k, gate_in=gate_in, gate_out=gate_out):
                for u in range(2):
                    at = i * 2 + u
                    at = steps - 1 - at if k == 0 else at
                    here = tile_rows(at)
                    delta = delta_ref[k, here, cols]
                    sig = sig_ref[here, cols]
                    weight = delta * sig
                    cot = cot_ref[here, cols]
                    by_in = jnp.zeros((SUB, LANES), F32)
                    by_decay = jnp.zeros((SUB, LANES), F32)
                    new = []
                    for n in range(depth):
                        adjoint = cot * gate_ref[gate_out + n, here, :] + carried[n]
                        by_in = by_in + adjoint * gate_ref[gate_in + n, here, :]
                        by_decay = by_decay + adjoint * (
                            keep_ref[at, n] * rate_ref[k * depth + n, :, cols]
                        )
                        lane = slice((gate_in + n) * LANES, (gate_in + n + 1) * LANES)
                        acc_ref[here, lane] += adjoint * weight
                        new.append(decay_ref[at, n] * adjoint)
                    gsig_ref[here, cols] += by_in * delta
                    gpre_ref[k, here, cols] = by_in * sig + by_decay * (1.0 / LOG2E)
                    carried = tuple(new)
                return carried

            lax.fori_loop(
                0, steps // 2, backward, tuple(start(1 - k, k, n, cols) for n in range(depth))
            )
        return 0

    lax.fori_loop(0, width // LANES, block_body, 0)

    skip = skip_ref[...]
    layer = (core_ref[...] + skip * sig_ref[...]).astype(BF16)
    out_ref[...] = mm(order_matrix(rows, True), layer).astype(BF16)
    base_ref[...] = gsig_ref[...] + skip * cot_ref[...]
    for k in range(2):
        slope = 1.0 / (1.0 + jnp.exp(-pre_ref[k]))
        grad_pre = (gpre_ref[k] * slope).astype(BF16)
        part_ref[:, k * rank : (k + 1) * rank] = lax.dot_general(
            grad_pre, wd_ref[k], NT, preferred_element_type=F32
        )
    gates = 4 * depth
    acc = acc_ref[...]
    high = acc.astype(BF16)
    low = (acc - high.astype(F32)).astype(BF16)
    lane = lax.broadcasted_iota(jnp.int32, (gates * LANES, gates), 0) >> 7
    column = lax.broadcasted_iota(jnp.int32, (gates * LANES, gates), 1)
    ones = jnp.where(lane == column, 1.0, 0.0).astype(BF16)
    part_ref[:, 2 * rank :] = mm(high, ones) + mm(low, ones)


def final_kernel(
    peers, part_ref, w_ref, base_ref, out_ref, slots_ref, send_sem, recv_sem
):
    greeting = greet(chan_places(peers))
    slots_ref[lax.axis_index("chan")] = part_ref[...]
    total, sends = share_and_sum(peers, slots_ref, send_sem, recv_sem, greeting)
    grad = mm(total.astype(BF16), w_ref[...]) + base_ref[...]
    out_ref[...] = mm(order_matrix(out_ref.shape[0], True), grad.astype(BF16)).astype(BF16)
    for copy in sends:
        copy.wait_send()


def shape(dims, dtype=F32):
    return jax.ShapeDtypeStruct(dims, dtype)


def call(kernel, out_shape, scratch, group=None):
    params = dict(vmem_limit_bytes=LIMIT)
    if group is not None:
        params.update(collective_id=group, has_side_effects=True)
    space = pl.BlockSpec(memory_space=pltpu.VMEM)

    def run(*args):
        return pl.pallas_call(
            kernel,
            out_shape=out_shape,
            in_specs=[space] * len(args),
            out_specs=jax.tree.map(lambda _: space, out_shape),
            scratch_shapes=scratch,
            compiler_params=pltpu.CompilerParams(**params),
        )(*args)

    return run


def local(sizes, signal, cotangent, w_proj, w_delta, delta_bias, decay_log, skip_gain):
    rows, width = signal.shape
    depth = decay_log.shape[1]
    steps = rows // SUB
    proj = w_proj.shape[1]
    gates = 4 * depth
    peers = sizes["chan"]
    levels = radices(sizes["seq"])
    vmem = lambda *dims: pltpu.VMEM(dims, F32)
    dma = lambda count: [pltpu.SemaphoreType.DMA((count,))] * 2
    w_turned = w_proj.T
    logs = decay_log.transpose(1, 0, 2)
    slots = [vmem(peers, rows, proj)] + dma(peers - 1)
    projected, sigp, cotp = call(
        functools.partial(project_kernel, peers),
        (shape((rows, proj), BF16), shape((rows, width), BF16), shape((rows, width), BF16)),
        slots,
        0,
    )(signal, cotangent, w_turned)
    common = [
        vmem(2, rows, width),
        vmem(rows, width),
        vmem(rows, width),
        vmem(gates, rows, LANES),
        vmem(2 * depth, SUB, width),
    ]
    pre, entry, span, dev, total = call(
        summary_kernel,
        (
            shape((2, rows, width)),
            shape((2, 2 * depth, SUB, width)),
            shape((2, 2, SUB, width)),
            shape((2, 2 * depth, width), BF16),
            shape((2, width)),
        ),
        common + [vmem(2, 2 * depth, width)],
    )(projected, sigp, cotp, w_delta, delta_bias, logs)
    enter = call(
        functools.partial(exchange_kernel, levels),
        shape((2, 2 * depth, width)),
        [
            [pltpu.VMEM((radix, 2, 2 * depth, width), BF16) for radix in levels],
            [vmem(radix, 2, width) for radix in levels],
            vmem(2 * depth, width),
            vmem(2, 2, width),
        ]
        + dma(2 * sum(radix - 1 for radix in levels)),
        1,
    )(logs, dev, total)
    layer_out, grad_part, base = call(
        scan_kernel,
        (shape((rows, width), BF16), shape((rows, proj)), shape((rows, width))),
        common
        + [
            vmem(rows, width),
            vmem(rows, width),
            vmem(2, rows, width),
            vmem(rows, gates * LANES),
            vmem(steps, depth, SUB, LANES),
            vmem(steps, depth, SUB, LANES),
        ],
    )(
        projected, sigp, cotp, pre, w_delta, logs, skip_gain.reshape(1, width),
        entry, span, enter,
    )
    signal_grad = call(
        functools.partial(final_kernel, peers), shape((rows, width), BF16), slots, 2
    )(grad_part, w_turned, base)
    return (layer_out, signal_grad)


def solution(mesh):
    in_specs = (
        P("seq", "chan"),
        P("seq", "chan"),
        P("chan", None),
        P(None, None, "chan"),
        P(None, "chan"),
        P(None, None, "chan"),
        P("chan"),
    )
    out_specs = (P("seq", "chan"), P("seq", "chan"))
    run = functools.partial(local, dict(mesh.shape))
    return jax.shard_map(run, mesh=mesh, in_specs=in_specs, out_specs=out_specs, check_vma=False)
```

profile of v0, /device:TPU:0, one launch (start us, length us, event | category | flops | bytes accessed | tf_op | source)
XLA Modules:
  0.0 64.7 jit_solution(3539644843150787164)
XLA Ops:
  0.6 4.6 %shard_map.86 = (bf16[128,560]{1,0:T(8,128)(2,1)}, bf16[128,1024]{1,0:T(8,128)(2,1)}, bf16[128,1024]{1,0:T(8,128)(2,1)}) custom-call(bf16[128,1024]{1,0:T(8,128)(2,1)} %sig_ref.1, bf16[128,1024]{1,0:T(8,128)(2,1)} %cot_ref.1, bf16[560,1024]{1,0:T(8,128)(2,1)} %bitcast.3), custom_call_target="tpu_custom_call" | custom-call | tf_op jit(solution)/shard_map/pallas_call | solution.py:451
  5.3 12.5 %shard_map.87 = (f32[2,128,1024]{2,1,0:T(8,128)}, f32[2,24,8,1024]{3,2,1,0:T(8,128)}, f32[2,2,8,1024]{3,2,1,0:T(8,128)}, bf16[2,24,1024]{2,1,0:T(8,128)(2,1)}, f32[2,1024]{1,0:T(2,128)}) custom-call(bf16[128,560]{1,0:T(8,128)(2,1)} %get-tuple-element.13.proj_ref, bf16[128,1024]{1,0:T(8,128)(2,1)} %get-tuple-element.14.sigp_ref, ...), custom_call_target="tpu_custom_call" | custom-call | tf_op jit(solution)/shard_map/pallas_call | solution.py:451
  17.8 20.7 %shard_map.88.enter_ref = f32[2,24,1024]{2,1,0:T(8,128)} custom-call(f32[12,2,1024]{2,1,0:T(2,128)} %bitcast.6, bf16[2,24,1024]{2,1,0:T(8,128)(2,1)} %get-tuple-element.19.dev_ref, f32[2,1024]{1,0:T(2,128)} %get-tuple-element.20.total_ref), custom_call_target="tpu_custom_call" | custom-call | tf_op jit(solution)/shard_map/pallas_call | solution.py:451
  38.5 20.2 %shard_map.89 = (bf16[128,1024]{1,0:T(8,128)(2,1)}, f32[128,560]{1,0:T(8,128)}, f32[128,1024]{1,0:T(8,128)}) custom-call(bf16[128,560]{1,0:T(8,128)(2,1)} %get-tuple-element.13.proj_ref, bf16[128,1024]{1,0:T(8,128)(2,1)} %get-tuple-element.14.sigp_ref, bf16[128,1024]{1,0:T(8,128)(2,1)} %get-tuple-element.15.cotp_ref, ...), custom_call_target="tpu_custom_call" | custom-call | tf_op jit(solution)/shard_map/pallas_call | solution.py:451
  58.7 4.4 %shard_map.90 = bf16[128,1024]{1,0:T(8,128)(2,1)} custom-call(f32[128,560]{1,0:T(8,128)} %get-tuple-element.22.part_ref, bf16[560,1024]{1,0:T(8,128)(2,1)} %bitcast.4, f32[128,1024]{1,0:T(8,128)} %get-tuple-element.23.base_ref), custom_call_target="tpu_custom_call" | custom-call | tf_op jit(solution)/shard_map/pallas_call | solution.py:451
  63.1 1.7 %copy.10 = bf16[128,1024]{1,0:T(8,128)(2,1)} copy(bf16[128,1024]{1,0:T(8,128)(2,1)} %shard_map.90) | data formatting | bytes 524288
where the time goes:
time: 65 us; the launch traced here: 64.7 us
  Pallas kernels  62.4 us (96%)
  local copies, waits for them, and re-layouts  1.67 us (3%)
  between operations  0.65 us (1%)
    pallas_call x5, Pallas kernels, run(): pl.pallas_call(kernel, out_shape=out_shape, in_specs=[space] * len(args),...  62.4 us
    unnamed x1, local copies, waits for them, and re-layouts  1.67 us

commit v1 on v0

v1 whole, which is shorter than its diff:
```python
import functools
import math

import jax
import jax.numpy as jnp
from jax import lax
from jax.experimental import pallas as pl
from jax.experimental.pallas import tpu as pltpu
from jax.sharding import PartitionSpec as P

SUB = 8
LANES = 128
MESH = pl.DeviceIdType.MESH
LIMIT = 56 * 1024 * 1024
F32 = jnp.float32
BF16 = jnp.bfloat16
LOG2E = math.log2(math.e)
NT = (((1,), (1,)), ((), ()))


def mm(a, b):
    return jnp.dot(a, b, preferred_element_type=F32)


def order_matrix(rows, back):
    steps = rows // SUB
    work, token = (1, 0) if back else (0, 1)
    r = lax.broadcasted_iota(jnp.int32, (rows, rows), work)
    t = lax.broadcasted_iota(jnp.int32, (rows, rows), token)
    return jnp.where(t == (r & (SUB - 1)) * steps + (r >> 3), 1.0, 0.0).astype(BF16)


def tile_rows(step):
    return pl.ds(pl.multiple_of(step * SUB, SUB), SUB)


def tile_cols(block):
    return pl.ds(pl.multiple_of(block * LANES, LANES), LANES)


def softplus(x):
    return jnp.maximum(x, 0.0) + jnp.log1p(jnp.exp(-jnp.abs(x)))


def fill_rates(log_ref, rate_ref):
    depth = log_ref.shape[0]
    for k in range(2):
        rate = jnp.exp(log_ref[:, k]) * (-LOG2E)
        for n in range(depth):
            rate_ref[k * depth + n] = jnp.broadcast_to(rate[n : n + 1], rate_ref.shape[1:])


def fill_gates(gates, gate_ref):
    for m in range(gate_ref.shape[0]):
        gate_ref[m] = jnp.broadcast_to(gates[:, m : m + 1], gate_ref.shape[1:])


def greet(places):
    barrier = pltpu.get_barrier_semaphore()
    for place in places:
        pl.semaphore_signal(barrier, inc=1, device_id=place, device_id_type=MESH)
    return barrier, len(places)


def share_and_sum(peers, slots_ref, send_sem, recv_sem, greeting):
    me = lax.axis_index("chan")
    pl.semaphore_wait(*greeting)
    sends = []
    for o in range(1, peers):
        copy = pltpu.make_async_remote_copy(
            src_ref=slots_ref.at[me],
            dst_ref=slots_ref.at[me],
            send_sem=send_sem.at[o - 1],
            recv_sem=recv_sem.at[o - 1],
            device_id={"chan": lax.rem(me + o, peers)},
            device_id_type=MESH,
        )
        copy.start()
        sends.append(copy)
    for o in range(1, peers):
        origin = lax.rem(me + peers - o, peers)
        pltpu.make_async_remote_copy(
            src_ref=slots_ref.at[origin],
            dst_ref=slots_ref.at[origin],
            send_sem=send_sem.at[o - 1],
            recv_sem=recv_sem.at[o - 1],
            device_id={"chan": origin},
            device_id_type=MESH,
        ).wait_recv()
    total = slots_ref[0]
    for p in range(1, peers):
        total = total + slots_ref[p]
    return total, sends


def chan_places(peers):
    me = lax.axis_index("chan")
    return [{"chan": lax.rem(me + o, peers)} for o in range(1, peers)]


def project_kernel(
    peers, sig_ref, cot_ref, w_ref, proj_ref, sigp_ref, cotp_ref, slots_ref, send_sem, recv_sem
):
    greeting = greet(chan_places(peers))
    me = lax.axis_index("chan")
    order = order_matrix(sig_ref.shape[0], False)
    sig = mm(order, sig_ref[...]).astype(BF16)
    slots_ref[me] = lax.dot_general(sig, w_ref[...], NT, preferred_element_type=F32)
    sigp_ref[...] = sig
    cotp_ref[...] = mm(order, cot_ref[...]).astype(BF16)
    total, sends = share_and_sum(peers, slots_ref, send_sem, recv_sem, greeting)
    proj_ref[...] = total.astype(BF16)
    for copy in sends:
        copy.wait_send()


def radices(count):
    found = []
    while count % 4 == 0 and count > 4:
        small = count % 16 == 0 and not found
        found += [2, 2] if small else [4]
        count //= 4
    return found + ([count] if count > 1 else [])


def place_at(me, stride, radix, shift):
    digit = lax.rem(me // stride, radix)
    return me + (lax.rem(digit + shift, radix) - digit) * stride


def sublane_scan(decay, value, rising):
    sub = lax.broadcasted_iota(jnp.int32, value.shape, 0)
    shift = 1
    while shift < SUB:
        amount = shift if rising else SUB - shift
        has = (sub >= shift) if rising else (sub < SUB - shift)
        value = value + decay * jnp.where(has, pltpu.roll(value, amount, 0), 0.0)
        decay = decay * jnp.where(has, pltpu.roll(decay, amount, 0), 1.0)
        shift *= 2
    edge = (sub >= 1) if rising else (sub < SUB - 1)
    before = jnp.where(edge, pltpu.roll(value, 1 if rising else SUB - 1, 0), 0.0)
    last = SUB - 1 if rising else 0
    return before, value[last : last + 1]


def core_kernel(
    levels, parts_count, span_lanes,
    proj_ref, sigp_ref, cotp_ref, wd_ref, bias_ref, log_ref, skip_ref,
    out_ref, part_ref, base_ref,
    delta_ref, slope_ref, sig_ref, cot_ref, gate_ref, rate_ref, stack_ref,
    entry_ref, span_ref, edge_ref, total_ref, enter_ref, wide_ref, run_ref,
    core_ref, gsig_ref, gpre_ref, acc_ref, keep_ref, decay_ref,
    part_refs, span_refs, send_sem, recv_sem,
):
    rows, width = sigp_ref.shape
    depth = log_ref.shape[0]
    rank = wd_ref.shape[1]
    steps = rows // SUB
    unroll = math.gcd(steps, 4)
    portion = width // parts_count
    me = lax.axis_index("seq")
    strides = [math.prod(levels[:i]) for i in range(len(levels))]
    greeting = greet(
        [
            {"seq": place_at(me, stride, radix, o)}
            for stride, radix in zip(strides, levels)
            for o in range(1, radix)
        ]
    )
    copies_each = 2 * sum(radix - 1 for radix in levels)
    sends = []

    proj = proj_ref[...]
    for k in range(2):
        pre = mm(proj[:, k * rank : (k + 1) * rank], wd_ref[k]) + bias_ref[k : k + 1, :]
        delta_ref[k] = softplus(pre)
        slope_ref[k] = 1.0 / (1.0 + jnp.exp(-pre))
    sig_ref[...] = sigp_ref[...].astype(F32)
    cot_ref[...] = cotp_ref[...].astype(F32)
    fill_gates(proj[:, 2 * rank :].astype(F32), gate_ref)
    fill_rates(log_ref, rate_ref)
    stack_ref[...] = jnp.exp(jnp.concatenate([log_ref[:, 0], log_ref[:, 1]], 0)) * (-LOG2E)

    def columns(unit):
        return pl.ds(pl.multiple_of(unit * span_lanes, span_lanes), span_lanes)

    def gate(m, here):
        one = gate_ref[m, here, :]
        return jnp.concatenate([one] * (span_lanes // LANES), 1)

    def fold_lanes(value):
        return sum(value[:, i : i + LANES] for i in range(0, span_lanes, LANES))

    def summarize(first_unit, end_unit):
        def unit_body(unit, _):
            cols = columns(unit)
            zero = jnp.zeros((SUB, span_lanes), F32)
            one = jnp.ones((SUB, span_lanes), F32)
            for k in range(2):
                for first in range(0, depth, 4):
                    ns = range(first, min(first + 4, depth))

                    def step_body(i, carry, ns=ns, k=k):
                        span, state, power, adjoint = carry
                        for u in range(unroll):
                            at = i * unroll + u
                            here = tile_rows(at if k == 0 else steps - 1 - at)
                            delta = delta_ref[k, here, cols]
                            weight = delta * sig_ref[here, cols]
                            cot = cot_ref[here, cols]
                            span = span + delta
                            new = ([], [], [])
                            for j, n in enumerate(ns):
                                a = jnp.exp2(delta * rate_ref[k * depth + n, :, cols])
                                p = a * power[j]
                                drive = weight * gate(2 * k * depth + n, here)
                                source = cot * gate((2 * k + 1) * depth + n, here)
                                new[0].append(a * state[j] + drive)
                                new[1].append(p)
                                new[2].append(adjoint[j] + p * source)
                            state, power, adjoint = (tuple(x) for x in new)
                        return span, state, power, adjoint

                    zeros = (zero,) * len(ns)
                    span, state, power, adjoint = lax.fori_loop(
                        0, steps // unroll, step_body, (zero, zeros, (one,) * len(ns), zeros)
                    )
                    if first == 0:
                        below, whole = sublane_scan(one, span, True)
                        above, _unused = sublane_scan(one, span, False)
                        span_ref[0, k, :, cols] = below
                        span_ref[1, k, :, cols] = above
                        total_ref[k : k + 1, cols] = whole
                    for j, n in enumerate(ns):
                        row = k * depth + n
                        for kind, value in ((0, state[j]), (1, adjoint[j])):
                            group = k ^ kind
                            before, edge = sublane_scan(power[j], value, group == 0)
                            entry_ref[group, row, :, cols] = before
                            edge_ref[group, row : row + 1, cols] = edge
            return 0

        if end_unit > first_unit:
            lax.fori_loop(first_unit, end_unit, unit_body, 0)

    def copies(level, q, slot, place, o, group):
        at = q * copies_each + 2 * sum(r - 1 for r in levels[:level]) + 2 * (o - 1)
        parts = part_refs[level].at[q]
        block = parts.at[slot, group] if level == len(levels) - 1 else parts.at[slot]
        return [
            pltpu.make_async_remote_copy(
                src_ref=ref,
                dst_ref=ref,
                send_sem=send_sem.at[at + i],
                recv_sem=recv_sem.at[at + i],
                device_id={"seq": place},
                device_id_type=MESH,
            )
            for i, ref in enumerate((block, span_refs[level].at[q, slot]))
        ]

    def digit_of(level):
        return lax.rem(me // strides[level], levels[level])

    def send(level, q):
        radix, digit = levels[level], digit_of(level)
        if level == 0:
            cols = slice(q * portion, (q + 1) * portion)
            part_refs[0][q, digit] = edge_ref[:, :, cols].astype(BF16)
            span_refs[0][q, digit] = total_ref[:, cols]
        for o in range(1, radix):
            peer = lax.rem(digit + o, radix)
            group = jnp.where(peer > digit, 0, 1)
            place = place_at(me, strides[level], radix, o)
            for copy in copies(level, q, digit, place, o, group):
                copy.start()
                sends.append(copy)

    def settle(level, q):
        radix, digit = levels[level], digit_of(level)
        last = level == len(levels) - 1
        cols = slice(q * portion, (q + 1) * portion)
        for o in range(1, radix):
            peer = lax.rem(digit + radix - o, radix)
            group = jnp.where(peer < digit, 0, 1)
            place = place_at(me, strides[level], radix, radix - o)
            for copy in copies(level, q, peer, place, o, group):
                copy.wait_recv()
        rates = stack_ref[:, cols]
        upper = lax.broadcasted_iota(jnp.int32, rates.shape, 0) < depth
        parts, spans = part_refs[level], span_refs[level]

        def power(span):
            return jnp.exp2(rates * jnp.where(upper, span[0:1], span[1:2]))

        for group in range(2):
            run_ref[...] = jnp.zeros_like(run_ref)
            far = jnp.zeros((2, portion), F32)
            if level == 0:
                enter_ref[group, :, cols] = jnp.zeros(rates.shape, F32)
                wide_ref[q, group] = far
            old = power(wide_ref[q, group])
            for step in range(radix):
                d = step if group == 0 else radix - 1 - step

                @pl.when(digit == d)
                def _(group=group, far=far, old=old):
                    enter_ref[group, :, cols] += old * run_ref[...]
                    wide_ref[q, group] += far

                def advance(d=d, group=group):
                    run_ref[...] = run_ref[...] * power(spans[q, d]) + parts[
                        q, d, group
                    ].astype(F32)

                if last:
                    pl.when((digit > d) if group == 0 else (digit < d))(advance)
                else:
                    advance()
                    far = far + spans[q, d]
            if not last:
                following = digit_of(level + 1)
                part_refs[level + 1][q, following, group] = run_ref[...].astype(BF16)
                if group == 0:
                    span_refs[level + 1][q, following] = far
        if not last:
            send(level + 1, q)

    def start(group, k, n, cols):
        row = k * depth + n
        decay = jnp.exp2(rate_ref[row, :, cols] * span_ref[group, k, :, cols])
        return entry_ref[group, row, :, cols] + decay * enter_ref[group, row : row + 1, cols]

    def gate_lanes(m):
        return slice(m * LANES, (m + 1) * LANES)

    def scan(first_unit, end_unit):
        def unit_body(unit, _):
            cols = columns(unit)
            for k in range(2):
                gate_in = 2 * k * depth
                gate_out = gate_in + depth

                def forward(i, states, k=k, gate_in=gate_in, gate_out=gate_out):
                    for u in range(unroll):
                        at = i * unroll + u
                        at = at if k == 0 else steps - 1 - at
                        here = tile_rows(at)
                        delta = delta_ref[k, here, cols]
                        weight = delta * sig_ref[here, cols]
                        cot = cot_ref[here, cols]
                        total = jnp.zeros((SUB, span_lanes), F32)
                        new = []
                        for n in range(depth):
                            a = jnp.exp2(delta * rate_ref[k * depth + n, :, cols])
                            kept = a * states[n]
                            h = kept + weight * gate(gate_in + n, here)
                            decay_ref[at, n] = a
                            keep_ref[at, n] = kept
                            total = total + gate(gate_out + n, here) * h
                            acc_ref[here, gate_lanes(gate_out + n)] += fold_lanes(cot * h)
                            new.append(h)
                        if k == 0:
                            core_ref[here, cols] = total
                        else:
                            core_ref[here, cols] += total
                        states = tuple(new)
                    return states

                lax.fori_loop(
                    0, steps // unroll, forward, tuple(start(k, k, n, cols) for n in range(depth))
                )

                def backward(i, carried, k=k, gate_in=gate_in, gate_out=gate_out):
                    for u in range(unroll):
                        at = i * unroll + u
                        at = steps - 1 - at if k == 0 else at
                        here = tile_rows(at)
                        delta = delta_ref[k, here, cols]
                        sig = sig_ref[here, cols]
                        weight = delta * sig
                        cot = cot_ref[here, cols]
                        by_in = jnp.zeros((SUB, span_lanes), F32)
                        by_decay = jnp.zeros((SUB, span_lanes), F32)
                        new = []
                        for n in range(depth):
                            adjoint = cot * gate(gate_out + n, here) + carried[n]
                            by_in = by_in + adjoint * gate(gate_in + n, here)
                            by_decay = by_decay + adjoint * (
                                keep_ref[at, n] * rate_ref[k * depth + n, :, cols]
                            )
                            acc_ref[here, gate_lanes(gate_in + n)] += fold_lanes(adjoint * weight)
                            new.append(decay_ref[at, n] * adjoint)
                        if k == 0:
                            gsig_ref[here, cols] = by_in * delta
                        else:
                            gsig_ref[here, cols] += by_in * delta
                        gpre_ref[k, here, cols] = by_in * sig + by_decay * (1.0 / LOG2E)
                        carried = tuple(new)
                    return carried

                lax.fori_loop(
                    0,
                    steps // unroll,
                    backward,
                    tuple(start(1 - k, k, n, cols) for n in range(depth)),
                )
            return 0

        if end_unit > first_unit:
            lax.fori_loop(first_unit, end_unit, unit_body, 0)

    half = portion // span_lanes
    mid = half // 2
    top = len(levels)
    summarize(0, half)
    pl.semaphore_wait(*greeting)
    send(0, 0)
    summarize(half, half + mid)
    settle(0, 0)
    summarize(half + mid, 2 * half)
    send(0, 1)
    acc_ref[...] = jnp.zeros_like(acc_ref)
    for level in range(1, top - 1):
        settle(level, 0)
    settle(0, 1)
    settle(top - 1, 0)
    scan(0, mid)
    for level in range(1, top - 1):
        settle(level, 1)
    scan(mid, half)
    settle(top - 1, 1)
    scan(half, 2 * half)

    skip = skip_ref[...]
    layer = (core_ref[...] + skip * sig_ref[...]).astype(BF16)
    out_ref[...] = mm(order_matrix(rows, True), layer).astype(BF16)
    base_ref[...] = gsig_ref[...] + skip * cot_ref[...]
    for k in range(2):
        grad_pre = (gpre_ref[k] * slope_ref[k]).astype(BF16)
        part_ref[:, k * rank : (k + 1) * rank] = lax.dot_general(
            grad_pre, wd_ref[k], NT, preferred_element_type=F32
        )
    gates = 4 * depth
    acc = acc_ref[...]
    high = acc.astype(BF16)
    low = (acc - high.astype(F32)).astype(BF16)
    lane = lax.broadcasted_iota(jnp.int32, (gates * LANES, gates), 0) >> 7
    column = lax.broadcasted_iota(jnp.int32, (gates * LANES, gates), 1)
    ones = jnp.where(lane == column, 1.0, 0.0).astype(BF16)
    part_ref[:, 2 * rank :] = mm(high, ones) + mm(low, ones)
    for copy in sends:
        copy.wait_send()


def final_kernel(
    peers, part_ref, w_ref, base_ref, out_ref, slots_ref, send_sem, recv_sem
):
    greeting = greet(chan_places(peers))
    slots_ref[lax.axis_index("chan")] = part_ref[...]
    total, sends = share_and_sum(peers, slots_ref, send_sem, recv_sem, greeting)
    grad = mm(total.astype(BF16), w_ref[...]) + base_ref[...]
    out_ref[...] = mm(order_matrix(out_ref.shape[0], True), grad.astype(BF16)).astype(BF16)
    for copy in sends:
        copy.wait_send()


def shape(dims, dtype=F32):
    return jax.ShapeDtypeStruct(dims, dtype)


def call(kernel, out_shape, scratch, group=None):
    params = dict(vmem_limit_bytes=LIMIT)
    if group is not None:
        params.update(collective_id=group, has_side_effects=True)
    space = pl.BlockSpec(memory_space=pltpu.VMEM)

    def run(*args):
        return pl.pallas_call(
            kernel,
            out_shape=out_shape,
            in_specs=[space] * len(args),
            out_specs=jax.tree.map(lambda _: space, out_shape),
            scratch_shapes=scratch,
            compiler_params=pltpu.CompilerParams(**params),
        )(*args)

    return run


def local(sizes, signal, cotangent, w_proj, w_delta, delta_bias, decay_log, skip_gain):
    rows, width = signal.shape
    depth = decay_log.shape[1]
    steps = rows // SUB
    proj = w_proj.shape[1]
    gates = 4 * depth
    peers = sizes["chan"]
    levels = radices(sizes["seq"])
    vmem = lambda *dims: pltpu.VMEM(dims, F32)
    dma = lambda count: [pltpu.SemaphoreType.DMA((count,))] * 2
    w_turned = w_proj.T
    logs = decay_log.transpose(1, 0, 2)
    slots = [vmem(peers, rows, proj)] + dma(peers - 1)
    projected, sigp, cotp = call(
        functools.partial(project_kernel, peers),
        (shape((rows, proj), BF16), shape((rows, width), BF16), shape((rows, width), BF16)),
        slots,
        0,
    )(signal, cotangent, w_turned)
    parts_count = 2
    portion = width // parts_count
    span_lanes = math.gcd(portion, 2 * LANES)
    layer_out, grad_part, base = call(
        functools.partial(core_kernel, levels, parts_count, span_lanes),
        (shape((rows, width), BF16), shape((rows, proj)), shape((rows, width))),
        [
            vmem(2, rows, width),
            vmem(2, rows, width),
            vmem(rows, width),
            vmem(rows, width),
            vmem(gates, rows, LANES),
            vmem(2 * depth, SUB, width),
            vmem(2 * depth, width),
            vmem(2, 2 * depth, SUB, width),
            vmem(2, 2, SUB, width),
            vmem(2, 2 * depth, width),
            vmem(2, width),
            vmem(2, 2 * depth, width),
            vmem(parts_count, 2, 2, portion),
            vmem(2 * depth, portion),
            vmem(rows, width),
            vmem(rows, width),
            vmem(2, rows, width),
            vmem(rows, gates * LANES),
            vmem(steps, depth, SUB, span_lanes),
            vmem(steps, depth, SUB, span_lanes),
            [pltpu.VMEM((parts_count, r, 2, 2 * depth, portion), BF16) for r in levels],
            [vmem(parts_count, r, 2, portion) for r in levels],
        ]
        + dma(parts_count * 2 * sum(r - 1 for r in levels)),
        1,
    )(projected, sigp, cotp, w_delta, delta_bias, logs, skip_gain.reshape(1, width))
    signal_grad = call(
        functools.partial(final_kernel, peers), shape((rows, width), BF16), slots, 2
    )(grad_part, w_turned, base)
    return (layer_out, signal_grad)


def solution(mesh):
    in_specs = (
        P("seq", "chan"),
        P("seq", "chan"),
        P("chan", None),
        P(None, None, "chan"),
        P(None, "chan"),
        P(None, None, "chan"),
        P("chan"),
    )
    out_specs = (P("seq", "chan"), P("seq", "chan"))
    run = functools.partial(local, dict(mesh.shape))
    return jax.shard_map(run, mesh=mesh, in_specs=in_specs, out_specs=out_specs, check_vma=False)
```

time: 65 us -> 47.1 us (0.72)
  Pallas kernels: 62.4 us -> 43.8 us
  local copies, waits for them, and re-layouts: 1.67 us -> 2.38 us
    pallas_call x5 -> x3, Pallas kernels: 62.4 us -> 43.8 us  [run(): pl.pallas_call(kernel, out_shape=out_shape, in_specs=[space] * len(args),...]
    unnamed x1 -> x4, local copies, waits for them, and re-layouts: 1.67 us -> 2.38 us
where the time goes in v1:
time: 47.1 us; the launch traced here: 46.8 us
  Pallas kernels  43.8 us (93%)
  local copies, waits for them, and re-layouts  2.38 us (5%)
  between operations  0.67 us (1%)
    pallas_call x3, Pallas kernels, run(): pl.pallas_call(kernel, out_shape=out_shape, in_specs=[space] * len(args),...  43.8 us
    unnamed x4, local copies, waits for them, and re-layouts  2.38 us

profile of v1, /device:TPU:0, one launch (start us, length us, event | category | flops | bytes accessed | tf_op | source)
XLA Modules:
  0.0 46.8 jit_solution(9544773831556704418)
XLA Ops:
  0.6 4.6 %shard_map.86 = (bf16[128,560]{1,0:T(8,128)(2,1)}, bf16[128,1024]{1,0:T(8,128)(2,1)}, bf16[128,1024]{1,0:T(8,128)(2,1)}) custom-call(bf16[128,1024]{1,0:T(8,128)(2,1)} %sig_ref.1, bf16[128,1024]{1,0:T(8,128)(2,1)} %cot_ref.1, bf16[560,1024]{1,0:T(8,128)(2,1)} %bitcast.3), custom_call_target="tpu_custom_call" | custom-call | tf_op jit(solution)/shard_map/pallas_call | solution.py:479
  5.3 34.7 %shard_map.87 = (bf16[128,1024]{1,0:T(8,128)(2,1)}, f32[128,560]{1,0:T(8,128)}, f32[128,1024]{1,0:T(8,128)}) custom-call(bf16[128,560]{1,0:T(8,128)(2,1)} %get-tuple-element.8.proj_ref, bf16[128,1024]{1,0:T(8,128)(2,1)} %get-tuple-element.9.sigp_ref, bf16[128,1024]{1,0:T(8,128)(2,1)} %get-tuple-element.10.cotp_ref, bf16[2,256,1024]{2,1,0:T(8,128)(2,1)} %wd_ref.1, ...), custom_call_target="tpu_custom_call" | custom-call | tf_op jit(solution)/shard_map/pallas_call | solution.py:479
  40.0 0.0 copy-start
  40.0 4.4 %shard_map.88 = bf16[128,1024]{1,0:T(8,128)(2,1)} custom-call(f32[128,560]{1,0:T(8,128)} %get-tuple-element.12.part_ref, bf16[560,1024]{1,0:T(8,128)(2,1)} %bitcast.4, f32[128,1024]{1,0:T(8,128)} %get-tuple-element.13.base_ref), custom_call_target="tpu_custom_call" | custom-call | tf_op jit(solution)/shard_map/pallas_call | solution.py:479
  44.4 0.0 copy-done
  44.4 0.7 %copy.11 = bf16[128,1024]{1,0:T(8,128)(2,1)} copy(bf16[128,1024]{1,0:T(8,128)(2,1)S(1)} %copy-done) | data formatting | bytes 524288
  45.2 1.7 %copy.12 = bf16[128,1024]{1,0:T(8,128)(2,1)} copy(bf16[128,1024]{1,0:T(8,128)(2,1)} %shard_map.88) | data formatting | bytes 524288
Async XLA Ops:
  40.0 4.4 %copy-start = (bf16[128,1024]{1,0:T(8,128)(2,1)S(1)}, bf16[128,1024]{1,0:T(8,128)(2,1)}, u32[]{:S(2)}) copy-start(bf16[128,1024]{1,0:T(8,128)(2,1)} %get-tuple-element.16) | copy-start | bytes 786436
